TPU v7x, 512 devices: a whole 4x8x8 slice. The times are simulated.
512 devices in a mesh: context: 64 (over z, y), tensor: 8 (over x, core).
Axes of the slice: x: 4, y: 8, z: 8, core: 2. Of those that a mesh axis runs over, the one named last changes fastest.
Arguments:
- queries: bfloat16 [65536, 2048], P(('context', 'tensor')), may hold values from -6 to 6
- key_rows: bfloat16 [65536, 2048], P(('context', 'tensor')), may hold values from -6 to 6
- value_rows: bfloat16 [65536, 2048], P(('context', 'tensor')), may hold values from -6 to 6
- grad_output: bfloat16 [65536, 2048], P(('context', 'tensor')), may hold values from -6 to 6
Outputs:
- attended: bfloat16 [65536, 2048], P(('context', 'tensor'))
- grad_queries: bfloat16 [65536, 2048], P(('context', 'tensor'))
- grad_keys: bfloat16 [65536, 2048], P(('context', 'tensor'))
- grad_values: bfloat16 [65536, 2048], P(('context', 'tensor'))
All inputs are finite; a program needn't handle non-finite values.
Results may differ from a plain program's by a relative error of at most 0.007.
Values may be sent and summed in bfloat16 or wider, within the bound.
A program may use at most 64 MiB of HBM per device.

v0:
```python
import jax
import jax.numpy as jnp
from jax import lax
from jax.sharding import Mesh
from jax.sharding import PartitionSpec as P

H = 16
DH = 128
CONTEXT = ("context_0", "context_1")
CONTEXT_TENSOR = ("context_0", "context_1", "tensor")


eps = 1e-06


def neutral_like(x, identity):
    return jnp.broadcast_to(jnp.asarray(identity, x.dtype), x.shape)


def entering(x, axes, combine, identity, reverse):
    before = start = neutral_like(x, identity)
    running = x
    for axis in reversed(axes):
        count, mine = (lax.axis_size(axis), lax.axis_index(axis))
        pieces = lax.all_gather(running, axis)
        inside, running = (start, start)
        for k in reversed(range(count)) if reverse else range(count):
            passed = k > mine if reverse else k < mine
            running = combine(running, pieces[k])
            inside = jnp.where(passed, running, inside)
        before = combine(inside, before)
    return before


def add_states(earlier, later):
    return earlier + later


def block_sums(left, right):
    return jnp.einsum("sjhd,sjhe->shde", left, right, preferred_element_type=jnp.float32)


def earlier_sums(terms):
    running = jnp.cumsum(terms, axis=0)
    return jnp.concatenate([jnp.zeros_like(terms[:1]), running[:-1]], axis=0)


def later_sums(terms):
    return jnp.flip(earlier_sums(jnp.flip(terms, 0)), 0)


def body(queries, key_rows, value_rows, grad_output):
    tensor = lax.axis_size("tensor")
    precise = lax.Precision.HIGHEST
    query_in, key_in, value_in, grad_in = (
        lax.all_to_all(queries, "tensor", split_axis=1, concat_axis=0, tiled=True),
        lax.all_to_all(key_rows, "tensor", split_axis=1, concat_axis=0, tiled=True),
        lax.all_to_all(value_rows, "tensor", split_axis=1, concat_axis=0, tiled=True),
        lax.all_to_all(grad_output, "tensor", split_axis=1, concat_axis=0, tiled=True),
    )
    heads_local = H // tensor
    block_rows = query_in.shape[0] // tensor
    shape_four = (tensor, block_rows, heads_local, DH)
    query_h = query_in.reshape(shape_four)
    key_h = key_in.reshape(shape_four)
    value_h = value_in.reshape(shape_four)
    positions = jnp.arange(block_rows, dtype=jnp.int32)
    causal = positions[:, None] >= positions[None, :]
    state_terms = block_sums(key_h, value_h)
    state_total = jnp.sum(state_terms, axis=0)
    carried = entering(state_total, CONTEXT, add_states, jnp.zeros_like(state_total), False)
    state = carried[None] + earlier_sums(state_terms)
    scores = jnp.einsum("sihd,sjhd->shij", query_h, key_h, preferred_element_type=jnp.float32)
    weights = jnp.where(causal, scores, 0.0).astype(jnp.bfloat16)
    attn = jnp.einsum("shij,sjhe->sihe", weights, value_h, preferred_element_type=jnp.float32)
    attn = attn + jnp.einsum(
        "sihd,shde->sihe", query_h.astype(jnp.float32), state, precision=precise
    )
    root_mean = jnp.sqrt(jnp.mean(attn * attn, axis=-1, keepdims=True) + eps)
    normed = attn / root_mean
    normed_out = normed.astype(jnp.bfloat16).reshape(tensor * block_rows, heads_local * DH)
    cotangent = grad_in.reshape(shape_four).astype(jnp.float32)
    d_attn = (
        (cotangent - normed * jnp.mean(cotangent * normed, axis=-1, keepdims=True)) / root_mean
    ).astype(jnp.bfloat16)
    grad_terms = block_sums(query_h, d_attn)
    grad_total = jnp.sum(grad_terms, axis=0)
    carried_back = entering(grad_total, CONTEXT, add_states, jnp.zeros_like(grad_total), True)
    suffix = carried_back[None] + later_sums(grad_terms)
    d_scores = jnp.einsum("sihe,sjhe->shij", d_attn, value_h, preferred_element_type=jnp.float32)
    d_weights = jnp.where(causal, d_scores, 0.0).astype(jnp.bfloat16)
    query_grad = jnp.einsum("shij,sjhd->sihd", d_weights, key_h, preferred_element_type=jnp.float32)
    query_grad = query_grad + jnp.einsum(
        "sihe,shde->sihd", d_attn.astype(jnp.float32), state, precision=precise
    )
    key_grad = jnp.einsum("shij,sihd->sjhd", d_weights, query_h, preferred_element_type=jnp.float32)
    key_grad = key_grad + jnp.einsum(
        "sjhe,shde->sjhd", value_h.astype(jnp.float32), suffix, precision=precise
    )
    value_grad = jnp.einsum("shij,sihe->sjhe", weights, d_attn, preferred_element_type=jnp.float32)
    value_grad = value_grad + jnp.einsum(
        "sjhd,shde->sjhe", key_h.astype(jnp.float32), suffix, precision=precise
    )
    flat_shape = (tensor * block_rows, heads_local * DH)
    grad_query = query_grad.astype(jnp.bfloat16).reshape(flat_shape)
    grad_key = key_grad.astype(jnp.bfloat16).reshape(flat_shape)
    grad_value = value_grad.astype(jnp.bfloat16).reshape(flat_shape)
    attended, grad_queries, grad_keys, grad_values = (
        lax.all_to_all(normed_out, "tensor", split_axis=0, concat_axis=1, tiled=True),
        lax.all_to_all(grad_query, "tensor", split_axis=0, concat_axis=1, tiled=True),
        lax.all_to_all(grad_key, "tensor", split_axis=0, concat_axis=1, tiled=True),
        lax.all_to_all(grad_value, "tensor", split_axis=0, concat_axis=1, tiled=True),
    )
    return (attended, grad_queries, grad_keys, grad_values)


def solution(mesh):
    split = Mesh(
        mesh.devices.reshape(8, 8, mesh.shape["tensor"]), ("context_0", "context_1", "tensor")
    )
    return jax.shard_map(
        body,
        mesh=split,
        in_specs=(
            P(CONTEXT_TENSOR, None),
            P(CONTEXT_TENSOR, None),
            P(CONTEXT_TENSOR, None),
            P(CONTEXT_TENSOR, None),
        ),
        out_specs=(
            P(CONTEXT_TENSOR, None),
            P(CONTEXT_TENSOR, None),
            P(CONTEXT_TENSOR, None),
            P(CONTEXT_TENSOR, None),
        ),
        check_vma=False,
    )
```

profile of v0, /device:TPU:1, one launch (start us, length us, event | category | flops | bytes accessed | tf_op | source)
XLA Modules:
  0.0 268.0 jit_solution(1507043081089021482)
XLA Ops:
  7.2 2.0 copy.47
  9.2 10.4 %all-to-all-start.1 = ((bf16[128,8,256]{0,2,1:T(8,128)(2,1)}), bf16[128,8,256]{0,2,1:T(8,128)(2,1)S(1)}, u32[]{:S(2)}, u32[]{:S(2)}) async-start(bf16[128,8,256]{0,2,1:T(8,128)(2,1)} %bitcast.3), calls=%async_computation.1 | async-start | bytes 1048576 | tf_op jit(solution)/shard_map/all_to_all | solution.py:57
  19.9 9.2 %all-to-all-done.1 = bf16[128,8,256]{0,2,1:T(8,128)(2,1)S(1)} async-done(((bf16[128,8,256]{0,2,1:T(8,128)(2,1)}), bf16[128,8,256]{0,2,1:T(8,128)(2,1)S(1)}, u32[]{:S(2)}, u32[]{:S(2)}) %all-to-all-start.1) | async-done | bytes 524320 | tf_op jit(solution)/shard_map/all_to_all | solution.py:57
  29.1 12.6 %all_to_all.137 = bf16[128,8,256]{0,2,1:T(8,128)(2,1)S(1)} all-to-all(bf16[128,8,256]{0,2,1:T(8,128)(2,1)S(1)} %bitcast.115), channel_id=1, replica_groups=mesh['context_0'=8,'context_1'=8,'tensor'=8] {'tensor'}, dimensions={1} | all-to-all | bytes 1048576 | tf_op jit(solution)/shard_map/all_to_all | solution.py:58
  41.7 1.1 fusion.21
  43.0 34.9 %all-gather.11.cloned.1.call-done = f32[16,128,128]{2,1,0:T(8,128)} async-done(((f32[2,128,128]{2,1,0:T(8,128)}), f32[16,128,128]{2,1,0:T(8,128)}) %all-gather.11.cloned.1.call-update) | async-done | bytes 1048592 | tf_op jit(solution)/shard_map/all_gather | solution.py:25
  77.9 2.0 fusion.17
  79.9 1.0 copy.46
  80.9 9.8 %all-to-all-start = ((bf16[128,8,256]{0,2,1:T(8,128)(2,1)}), bf16[128,8,256]{0,2,1:T(8,128)(2,1)S(1)}, u32[]{:S(2)}, u32[]{:S(2)}) async-start(bf16[128,8,256]{0,2,1:T(8,128)(2,1)} %bitcast), calls=%async_computation | async-start | bytes 1048576 | tf_op jit(solution)/shard_map/all_to_all | solution.py:56
  90.8 1.0 copy.82
  91.8 1.1 fusion.23
  92.9 7.3 %all-to-all-done = bf16[128,8,256]{0,2,1:T(8,128)(2,1)S(1)} async-done(((bf16[128,8,256]{0,2,1:T(8,128)(2,1)}), bf16[128,8,256]{0,2,1:T(8,128)(2,1)S(1)}, u32[]{:S(2)}, u32[]{:S(2)}) %all-to-all-start) | async-done | bytes 524320 | tf_op jit(solution)/shard_map/all_to_all | solution.py:56
  100.2 4.9 %all-to-all-start.4 = ((bf16[128,8,256]{0,2,1:T(8,128)(2,1)}), bf16[128,8,256]{0,2,1:T(8,128)(2,1)}, u32[]{:S(2)}, u32[]{:S(2)}) async-start(bf16[128,8,256]{0,2,1:T(8,128)(2,1)} %bitcast.20), calls=%async_computation.4 | async-start | bytes 1048576 | tf_op jit(solution)/shard_map/all_to_all | solution.py:59
  105.1 1.1 fusion.4
  106.3 15.4 %all-gather.7.cloned.1.call-done = f32[8,2,128,128]{3,2,1,0:T(8,128)} async-done(((f32[1,2,128,128]{3,2,1,0:T(8,128)}), f32[8,2,128,128]{3,2,1,0:T(8,128)}) %all-gather.7.cloned.1.call-update) | async-done | bytes 1048592 | tf_op jit(solution)/shard_map/all_gather | solution.py:25
  121.7 1.5 fusion.16
  123.2 1.0 convolution_bitcast_fusion.6
  124.3 0.5 multiply_reduce_fusion.1
  124.8 1.2 multiply_reduce_fusion
  126.0 2.1 divide_convert_fusion
  128.2 0.5 fusion.22
  128.6 0.8 copy.61
  129.5 38.7 %all-gather.13.cloned.1.call-done = f32[16,128,128]{2,1,0:T(8,128)} async-done(((f32[2,128,128]{2,1,0:T(8,128)}), f32[16,128,128]{2,1,0:T(8,128)}) %all-gather.13.cloned.1.call-update) | async-done | bytes 1048592 | tf_op jit(solution)/shard_map/all_gather | solution.py:25
  168.2 2.0 fusion.13
  170.3 9.7 %all-to-all-start.3 = ((bf16[8,128,256]{1,2,0:T(8,128)(2,1)}), bf16[8,128,256]{1,2,0:T(8,128)(2,1)}, u32[]{:S(2)}, u32[]{:S(2)}) async-start(bf16[8,128,256]{1,2,0:T(8,128)(2,1)} %bitcast.112), calls=%async_computation.3 | async-start | bytes 1048576 | tf_op jit(solution)/shard_map/all_to_all | solution.py:109
  180.0 1.1 rev.7
  181.0 1.3 fusion.24
  182.4 1.1 concatenate.7
  183.9 0.8 copy-done.1
  184.7 0.6 convolution_bitcast_fusion.5
  185.5 1.3 fusion.6
  186.8 1.3 fusion.25
  188.0 23.7 %all-gather.9.cloned.1.call-done = f32[8,2,128,128]{3,2,1,0:T(8,128)} async-done(((f32[1,2,128,128]{3,2,1,0:T(8,128)}), f32[8,2,128,128]{3,2,1,0:T(8,128)}) %all-gather.9.cloned.1.call-update) | async-done | bytes 1048592 | tf_op jit(solution)/shard_map/all_gather | solution.py:25
  211.7 1.4 fusion.12
  213.2 9.5 %all-to-all-start.5 = ((bf16[8,128,256]{1,2,0:T(8,128)(2,1)}), bf16[8,128,256]{1,2,0:T(8,128)(2,1)S(1)}, u32[]{:S(2)}, u32[]{:S(2)}) async-start(bf16[8,128,256]{1,2,0:T(8,128)(2,1)} %bitcast.26), calls=%async_computation.5 | async-start | bytes 1048576 | tf_op jit(solution)/shard_map/all_to_all | solution.py:110
  222.7 1.4 reverse_add_fusion
  224.3 1.5 fusion.3
  225.7 6.5 %all-to-all-done.5 = bf16[8,128,256]{1,2,0:T(8,128)(2,1)S(1)} async-done(((bf16[8,128,256]{1,2,0:T(8,128)(2,1)}), bf16[8,128,256]{1,2,0:T(8,128)(2,1)S(1)}, u32[]{:S(2)}, u32[]{:S(2)}) %all-to-all-start.5) | async-done | bytes 524320 | tf_op jit(solution)/shard_map/all_to_all | solution.py:110
  232.2 4.9 %all-to-all-start.7 = ((bf16[8,128,256]{1,2,0:T(8,128)(2,1)}), bf16[8,128,256]{1,2,0:T(8,128)(2,1)}, u32[]{:S(2)}, u32[]{:S(2)}) async-start(bf16[8,128,256]{1,2,0:T(8,128)(2,1)} %bitcast.116), calls=%async_computation.7 | async-start | bytes 1048576 | tf_op jit(solution)/shard_map/all_to_all | solution.py:112
  237.1 1.0 convolution_bitcast_fusion.4
  238.1 1.1 fusion.7
  239.2 7.5 %all-to-all-done.7 = bf16[8,128,256]{1,2,0:T(8,128)(2,1)} async-done(((bf16[8,128,256]{1,2,0:T(8,128)(2,1)}), bf16[8,128,256]{1,2,0:T(8,128)(2,1)}, u32[]{:S(2)}, u32[]{:S(2)}) %all-to-all-start.7) | async-done | bytes 524320 | tf_op jit(solution)/shard_map/all_to_all | solution.py:112
  246.7 4.3 %all-to-all-start.6 = ((bf16[8,128,256]{1,2,0:T(8,128)(2,1)}), bf16[8,128,256]{1,2,0:T(8,128)(2,1)S(1)}, u32[]{:S(2)}, u32[]{:S(2)}) async-start(bf16[8,128,256]{1,2,0:T(8,128)(2,1)} %bitcast.35), calls=%async_computation.6 | async-start | bytes 1048576 | tf_op jit(solution)/shard_map/all_to_all | solution.py:111
  251.0 2.0 copy.81
  253.0 1.0 copy.83
  254.0 2.0 copy.85
  256.1 4.4 %all-to-all-done.6 = bf16[8,128,256]{1,2,0:T(8,128)(2,1)S(1)} async-done(((bf16[8,128,256]{1,2,0:T(8,128)(2,1)}), bf16[8,128,256]{1,2,0:T(8,128)(2,1)S(1)}, u32[]{:S(2)}, u32[]{:S(2)}) %all-to-all-start.6) | async-done | bytes 524320 | tf_op jit(solution)/shard_map/all_to_all | solution.py:111
  260.5 1.0 copy.84
  (47 shorter events, 1.5 us)
Async XLA Ops:
  9.2 10.4 %copy-start.12 = (bf16[128,2048]{1,0:T(8,128)(2,1)S(1)}, bf16[128,2048]{1,0:T(8,128)(2,1)}, u32[]{:S(2)}) copy-start(bf16[128,2048]{1,0:T(8,128)(2,1)} %param.6) | copy-start | bytes 1572868
  9.2 19.9 %all-to-all-start.1 = ((bf16[128,8,256]{0,2,1:T(8,128)(2,1)}), bf16[128,8,256]{0,2,1:T(8,128)(2,1)S(1)}, u32[]{:S(2)}, u32[]{:S(2)}) async-start(bf16[128,8,256]{0,2,1:T(8,128)(2,1)} %bitcast.3), calls=%async_computation.1 | async-start | bytes 1048576 | tf_op jit(solution)/shard_map/all_to_all | solution.py:57
  19.6 58.3 %all-gather.11.cloned.1.call-start = ((), (), s32[]{:S(2)}) async-start(), calls=%async_computation.10 | async-start | bytes 1179648 | tf_op jit(solution)/shard_map/all_gather | solution.py:25
  42.9 37.0 %copy-start.13 = (bf16[128,2048]{1,0:T(8,128)(2,1)S(1)}, bf16[128,2048]{1,0:T(8,128)(2,1)}, u32[]{:S(2)}) copy-start(bf16[128,2048]{1,0:T(8,128)(2,1)} %param.4) | copy-start | bytes 1572868
  42.9 78.7 %all-gather.7.cloned.1.call-start = ((), (), s32[]{:S(2)}) async-start(), calls=%async_computation.8 | async-start | bytes 1179648 | tf_op jit(solution)/shard_map/all_gather | solution.py:25
  80.9 9.8 %copy-start.14 = (bf16[128,2048]{1,0:T(8,128)(2,1)S(1)}, bf16[128,2048]{1,0:T(8,128)(2,1)}, u32[]{:S(2)}) copy-start(bf16[128,2048]{1,0:T(8,128)(2,1)} %param.7) | copy-start | bytes 1572868
  80.9 19.3 %all-to-all-start = ((bf16[128,8,256]{0,2,1:T(8,128)(2,1)}), bf16[128,8,256]{0,2,1:T(8,128)(2,1)S(1)}, u32[]{:S(2)}, u32[]{:S(2)}) async-start(bf16[128,8,256]{0,2,1:T(8,128)(2,1)} %bitcast), calls=%async_computation | async-start | bytes 1048576 | tf_op jit(solution)/shard_map/all_to_all | solution.py:56
  92.9 30.2 %copy-start = (f32[7,2,128,128]{3,2,1,0:T(8,128)}, f32[7,2,128,128]{3,2,1,0:T(8,128)S(1)}, u32[]{:S(2)}) copy-start(f32[7,2,128,128]{3,2,1,0:T(8,128)S(1)} %slice.168) | copy-start | bytes 2752516
  100.2 24.6 %all-to-all-start.4 = ((bf16[128,8,256]{0,2,1:T(8,128)(2,1)}), bf16[128,8,256]{0,2,1:T(8,128)(2,1)}, u32[]{:S(2)}, u32[]{:S(2)}) async-start(bf16[128,8,256]{0,2,1:T(8,128)(2,1)} %bitcast.20), calls=%async_computation.4 | async-start | bytes 1048576 | tf_op jit(solution)/shard_map/all_to_all | solution.py:59
  105.1 16.5 %copy-start.7 = (f32[16,128,128]{2,1,0:T(8,128)S(1)}, f32[16,128,128]{2,1,0:T(8,128)}, u32[]{:S(2)}) copy-start(f32[16,128,128]{2,1,0:T(8,128)} %all-gather.11.cloned.1.call-done) | copy-start | bytes 3145732
  105.1 63.1 %all-gather.13.cloned.1.call-start = ((), (), s32[]{:S(2)}) async-start(), calls=%async_computation.11 | async-start | bytes 1179648 | tf_op jit(solution)/shard_map/all_gather | solution.py:25
  123.1 1.0 copy-start.9
  123.2 1.1 copy-start.4
  129.4 82.3 %all-gather.9.cloned.1.call-start = ((), (), s32[]{:S(2)}) async-start(), calls=%async_computation.9 | async-start | bytes 1179648 | tf_op jit(solution)/shard_map/all_gather | solution.py:25
  170.3 42.9 %all-to-all-start.3 = ((bf16[8,128,256]{1,2,0:T(8,128)(2,1)}), bf16[8,128,256]{1,2,0:T(8,128)(2,1)}, u32[]{:S(2)}, u32[]{:S(2)}) async-start(bf16[8,128,256]{1,2,0:T(8,128)(2,1)} %bitcast.112), calls=%async_computation.3 | async-start | bytes 1048576 | tf_op jit(solution)/shard_map/all_to_all | solution.py:109
  183.5 1.2 copy-start.1
  183.5 1.2 copy-start.10
  184.7 0.8 copy-start.2
  185.5 1.3 copy-start.5
  186.7 24.9 %copy-start.8 = (f32[16,128,128]{2,1,0:T(8,128)S(1)}, f32[16,128,128]{2,1,0:T(8,128)}, u32[]{:S(2)}) copy-start(f32[16,128,128]{2,1,0:T(8,128)} %all-gather.13.cloned.1.call-done) | copy-start | bytes 3145732
  186.7 24.9 %copy-start.11 = (f32[1,2,128,128]{3,2,1,0:T(8,128)S(1)}, f32[1,2,128,128]{3,2,1,0:T(8,128)}, u32[]{:S(2)}) copy-start(f32[1,2,128,128]{3,2,1,0:T(8,128)} %get-tuple-element.4) | copy-start | bytes 393220
  213.2 19.0 %all-to-all-start.5 = ((bf16[8,128,256]{1,2,0:T(8,128)(2,1)}), bf16[8,128,256]{1,2,0:T(8,128)(2,1)S(1)}, u32[]{:S(2)}, u32[]{:S(2)}) async-start(bf16[8,128,256]{1,2,0:T(8,128)(2,1)} %bitcast.26), calls=%async_computation.5 | async-start | bytes 1048576 | tf_op jit(solution)/shard_map/all_to_all | solution.py:110
  222.7 1.5 copy-start.6
  232.2 14.5 %all-to-all-start.7 = ((bf16[8,128,256]{1,2,0:T(8,128)(2,1)}), bf16[8,128,256]{1,2,0:T(8,128)(2,1)}, u32[]{:S(2)}, u32[]{:S(2)}) async-start(bf16[8,128,256]{1,2,0:T(8,128)(2,1)} %bitcast.116), calls=%async_computation.7 | async-start | bytes 1048576 | tf_op jit(solution)/shard_map/all_to_all | solution.py:112
  237.1 1.0 copy-start.3
  246.7 13.8 %all-to-all-start.6 = ((bf16[8,128,256]{1,2,0:T(8,128)(2,1)}), bf16[8,128,256]{1,2,0:T(8,128)(2,1)S(1)}, u32[]{:S(2)}, u32[]{:S(2)}) async-start(bf16[8,128,256]{1,2,0:T(8,128)(2,1)} %bitcast.35), calls=%async_computation.6 | async-start | bytes 1048576 | tf_op jit(solution)/shard_map/all_to_all | solution.py:111
Sparse Core Ops, SparseCore 0:
  43.0 34.8 all-gather.10
  80.5 41.0 all-gather.6
  129.5 38.6 all-gather.12
  170.4 41.2 all-gather.8
where the time goes:
time: 269 us; the launch traced here: 268 us
  waiting for transfers between devices  148 us (55%)
  starting transfers between devices  53.5 us (20%)
  local copies, waits for them, and re-layouts  14.8 us (6%)
  other arithmetic  14.1 us (5%)
  between operations  14 us (5%)
  blocking collectives  12.6 us (5%)
  matrix products  11.3 us (4%)
    all_gather x4, waiting for transfers between devices, entering(): pieces = lax.all_gather(running, axis)  113 us
    all_to_all x1, blocking collectives, body(): lax.all_to_all(value_rows, 'tensor', split_axis=1, concat_axis=0, tiled=T...  12.6 us
    all_to_all x1, starting transfers between devices, body(): lax.all_to_all(key_rows, 'tensor', split_axis=1, concat_axis=0, tiled=True)  10.4 us
    all_to_all x1, starting transfers between devices, body(): lax.all_to_all(queries, 'tensor', split_axis=1, concat_axis=0, tiled=True)  9.8 us
    all_to_all x1, starting transfers between devices, body(): lax.all_to_all(normed_out, 'tensor', split_axis=0, concat_axis=1, tiled=T...  9.68 us
    all_to_all x1, starting transfers between devices, body(): lax.all_to_all(grad_query, 'tensor', split_axis=0, concat_axis=1, tiled=T...  9.5 us
    all_to_all x1, waiting for transfers between devices, body(): lax.all_to_all(key_rows, 'tensor', split_axis=1, concat_axis=0, tiled=True)  9.22 us
    all_to_all x1, waiting for transfers between devices, body(): lax.all_to_all(grad_value, 'tensor', split_axis=0, concat_axis=1, tiled=T...  7.48 us
  transfers between devices with their start and end apart: 11, of which 9 were waited for; matrix products, arithmetic and copies ran while one was open for 10% of the time, Pallas kernels for 0%

commit v1 on v0

v1 whole, which is shorter than its diff:
```python
import jax
import jax.numpy as jnp
from jax import lax
from jax.experimental import pallas as pl
from jax.experimental.pallas import tpu as pltpu
from jax.sharding import PartitionSpec as P

DH = 128
NZ, NY, NX, NC = 8, 8, 4, 2
STREAMS = 2
EPS = 1e-06
MESH = pl.DeviceIdType.MESH
F32 = jnp.float32
BF16 = jnp.bfloat16


def dot(a, b, ca, cb):
    return lax.dot_general(a, b, (((ca,), (cb,)), ((), ())), preferred_element_type=F32)


def kernel(
    q_in, k_in, v_in, g_in, att_out, gq_out, gk_out, gv_out,
    q, k, v, g, w, local, da, att, gq, gk, gv, gkl, gvl, own_pre,
    cu_s, cu_r, mine, xu_s, xu_r, xpre, yu_s, yu_r, ypre, z_s, z_r,
    yd_s, yd_r, xd_s, xd_r, cd_s, cd_r, ssem, rsem, io_sem,
):
    rows = q.shape[0]
    ctx, ten = lax.axis_index("context"), lax.axis_index("tensor")
    z, y = ctx // NY, lax.rem(ctx, NY)
    x, c = ten // NC, lax.rem(ten, NC)
    peer = 1 - c

    def at_core():
        return (ctx, x * NC + peer)

    def at_x(i):
        return (ctx, i * NC + c)

    def at_y(i):
        return (z * NY + i, ten)

    def at_z(i):
        return (i * NY + y, ten)

    rings = ((at_x, x, NX), (at_y, y, NY), (at_z, z, NZ))
    barrier = pltpu.get_barrier_semaphore()
    pl.semaphore_signal(barrier, inc=1, device_id=at_core(), device_id_type=MESH)
    for place, me, n in rings:
        for off in range(1, n):
            pl.semaphore_signal(
                barrier, inc=1, device_id=place(lax.rem(me + off, n)), device_id_type=MESH
            )

    loads = []
    for i, (src, dst) in enumerate(((k_in, k), (v_in, v), (q_in, q), (g_in, g))):
        loads.append(pltpu.make_async_copy(src, dst, io_sem.at[i]))
        loads[-1].start()

    row_id = lax.broadcasted_iota(jnp.int32, (rows, rows), 0)
    col_id = lax.broadcasted_iota(jnp.int32, (rows, rows), 1)
    causal = row_id >= col_id

    def cols(h):
        return pl.ds(pl.multiple_of(h * DH, DH), DH)

    def head(core, i, s):
        return core * (NX * STREAMS) + i * STREAMS + s

    def copy(src, dst, d, s, r, to):
        return pltpu.make_async_remote_copy(
            src_ref=src, dst_ref=dst, send_sem=ssem.at[d, s, r], recv_sem=rsem.at[d, s, r],
            device_id=to, device_id_type=MESH,
        )

    pending = []

    def scatter(src, dst, d, s, r, ring, whole=False):
        place, me, n = rings[ring]
        for off in range(1, n):
            to = lax.rem(me + off, n)
            copy(src if whole else src.at[to], dst.at[me], d, s, r, place(to)).start()

        def all_of():
            part = dst.at[pl.ds(0, n - 1)]
            return copy(part, part, d, s, r, place(lax.rem(me + 1, n)))

        pending.append(all_of)
        return all_of

    def settle():
        for p in pending:
            p().wait_send()
        pending.clear()

    waits = {}

    def term(d, h):
        if d == 0:
            return dot(k[:, cols(h)], v[:, cols(h)], 0, 0)
        return dot(q[:, cols(h)], da[:, cols(h)], 0, 0)

    def core_up(d, s):
        for i in range(NX):
            cu_s[d, s, i] = term(d, head(peer, i, s)).astype(BF16)
        return lambda: None

    def core_up_send(d, s):
        def whole():
            return copy(cu_s.at[d, s], cu_r.at[d, s], d, s, 0, at_core())

        whole().start()
        pending.append(whole)
        waits[d, s, 0] = whole
        for i in range(NX):
            mine[d, s, i] = term(d, head(c, i, s))

    def x_up(d, s):
        waits[d, s, 0]().wait_recv()
        for i in range(NX):
            xu_s[d, s, i] = (mine[d, s, i] + cu_r[d, s, i].astype(F32)).astype(BF16)
        waits[d, s, 1] = scatter(xu_s.at[d, s], xu_r.at[d, s], d, s, 1, 0)
        xu_r[d, s, x] = xu_s[d, s, x]

    def order(d, n):
        return range(n) if d == 0 else range(n - 1, -1, -1)

    def y_up(d, s):
        waits[d, s, 1]().wait_recv()
        run = jnp.zeros((DH, DH), F32)
        for i in order(d, NX):
            xpre[d, s, i] = run
            run = run + xu_r[d, s, i].astype(F32)
        yu_s[d, s] = run.astype(BF16).reshape(NY, DH // NY, DH)
        waits[d, s, 2] = scatter(yu_s.at[d, s], yu_r.at[d, s], d, s, 2, 1)
        yu_r[d, s, y] = yu_s[d, s, y]

    def z_all(d, s):
        waits[d, s, 2]().wait_recv()
        run = jnp.zeros((DH // NY, DH), F32)
        for i in order(d, NY):
            ypre[d, s, i] = run
            run = run + yu_r[d, s, i].astype(F32)
        z_s[d, s] = run.astype(z_s.dtype)
        waits[d, s, 3] = scatter(z_s.at[d, s], z_r.at[d, s], d, s, 3, 2, whole=True)
        z_r[d, s, z] = z_s[d, s]

    def y_down(d, s):
        waits[d, s, 3]().wait_recv()
        base = jnp.zeros((DH // NY, DH), F32)
        for i in range(NZ):
            passed = i < z if d == 0 else i > z
            base = base + jnp.where(passed, z_r[d, s, i].astype(F32), 0.0)
        for i in range(NY):
            yd_s[d, s, i] = (base + ypre[d, s, i]).astype(BF16)
        waits[d, s, 4] = scatter(yd_s.at[d, s], yd_r.at[d, s], d, s, 4, 1)
        yd_r[d, s, y] = yd_s[d, s, y]

    def x_down(d, s):
        waits[d, s, 4]().wait_recv()
        base = yd_r[d, s].reshape(DH, DH).astype(F32)
        for i in range(NX):
            xd_s[d, s, i] = (base + xpre[d, s, i]).astype(BF16)
        waits[d, s, 5] = scatter(xd_s.at[d, s], xd_r.at[d, s], d, s, 5, 0)
        xd_r[d, s, x] = xd_s[d, s, x]

    def core_down(d, s):
        waits[d, s, 5]().wait_recv()
        first = 0 if d == 0 else 1
        for i in range(NX):
            chip = xd_r[d, s, i].astype(F32)
            cd_s[d, s, i] = (chip + jnp.where(c == first, mine[d, s, i], 0.0)).astype(BF16)
            own_pre[d, s, i] = (
                chip + jnp.where(c == first, 0.0, cu_r[d, s, i].astype(F32))
            ).astype(BF16)

        def whole():
            return copy(cd_s.at[d, s], cd_r.at[d, s], d, s, 6, at_core())

        whole().start()
        pending.append(whole)
        waits[d, s, 6] = whole

    def local_forward(core, s):
        for i in range(NX):
            h = head(core, i, s)
            sc = dot(q[:, cols(h)], k[:, cols(h)], 1, 1)
            wt = jnp.where(causal, sc, 0.0).astype(BF16)
            w[h] = wt
            local[:, cols(h)] = dot(wt, v[:, cols(h)], 1, 0)

    def normalize(core, s, state):
        for i in range(NX):
            h = head(core, i, s)
            a = local[:, cols(h)] + dot(q[:, cols(h)], state[0, s, i], 1, 0)
            inv = lax.rsqrt(jnp.mean(a * a, axis=-1, keepdims=True) + EPS)
            normed = a * inv
            att[:, cols(h)] = normed.astype(BF16)
            cot = g[:, cols(h)].astype(F32)
            m = jnp.mean(cot * normed, axis=-1, keepdims=True)
            da[:, cols(h)] = ((cot - normed * m) * inv).astype(BF16)

    def local_backward(core, s, state):
        for i in range(NX):
            h = head(core, i, s)
            d_a = da[:, cols(h)]
            dw = jnp.where(causal, dot(d_a, v[:, cols(h)], 1, 1), 0.0).astype(BF16)
            gq[:, cols(h)] = (
                dot(dw, k[:, cols(h)], 1, 0) + dot(d_a, state[0, s, i], 1, 1)
            ).astype(BF16)
            gkl[:, cols(h)] = dot(dw, q[:, cols(h)], 0, 0)
            gvl[:, cols(h)] = dot(w[h], d_a, 0, 0)

    def finish(core, s, state):
        for i in range(NX):
            h = head(core, i, s)
            suf = state[1, s, i]
            gk[:, cols(h)] = (gkl[:, cols(h)] + dot(v[:, cols(h)], suf, 1, 1)).astype(BF16)
            gv[:, cols(h)] = (gvl[:, cols(h)] + dot(k[:, cols(h)], suf, 1, 0)).astype(BF16)

    streams = range(STREAMS)
    middle = (x_up, y_up, z_all, y_down, x_down, core_down)

    loads[0].wait()
    loads[1].wait()
    for s in streams:
        core_up(0, s)
        if s == 0:
            pl.semaphore_wait(barrier, 1 + (NX - 1) + (NY - 1) + (NZ - 1))
        core_up_send(0, s)
    loads[2].wait()
    loads[3].wait()
    work = [(core, s) for s in streams for core in (c, peer)]
    for j, stage in enumerate(middle):
        for s in streams:
            stage(0, s)
        if j < len(work):
            local_forward(*work[j])
    settle()
    for s in streams:
        normalize(c, s, own_pre)
        waits[0, s, 6]().wait_recv()
        normalize(peer, s, cd_r)
        core_up(1, s)
        core_up_send(1, s)
    att_copy = pltpu.make_async_copy(att, att_out, io_sem.at[4])
    att_copy.start()
    for j, stage in enumerate(middle):
        for s in streams:
            stage(1, s)
        if j < len(work):
            core, s = work[j]
            local_backward(core, s, own_pre if core is c else cd_r)
        if j + 1 == len(work):
            gq_copy = pltpu.make_async_copy(gq, gq_out, io_sem.at[5])
            gq_copy.start()
    settle_later = list(pending)
    for s in streams:
        finish(c, s, own_pre)
        waits[1, s, 6]().wait_recv()
        finish(peer, s, cd_r)
    gk_copy = pltpu.make_async_copy(gk, gk_out, io_sem.at[6])
    gv_copy = pltpu.make_async_copy(gv, gv_out, io_sem.at[7])
    gk_copy.start()
    gv_copy.start()
    settle()
    att_copy.wait()
    gq_copy.wait()
    gk_copy.wait()
    gv_copy.wait()


def body(queries, key_rows, value_rows, grad_output):
    rows, feats = queries.shape
    heads = feats // DH
    per = (2, STREAMS)
    full = (rows, feats)
    chunk = DH // NY

    def vm(shape, dtype):
        return pltpu.VMEM(shape, dtype)

    scratch = (
        [vm(full, BF16)] * 4
        + [vm((heads, rows, rows), BF16), vm(full, F32), vm(full, BF16)]
        + [vm(full, BF16)] * 4
        + [vm(full, F32)] * 2
        + [vm(per + (NX, DH, DH), BF16)]
        + [vm(per + (NX, DH, DH), BF16)] * 2
        + [vm(per + (NX, DH, DH), F32)]
        + [vm(per + (NX, DH, DH), BF16)] * 2
        + [vm(per + (NX, DH, DH), F32)]
        + [vm(per + (NY, chunk, DH), BF16)] * 2
        + [vm(per + (NY, chunk, DH), F32)]
        + [vm(per + (chunk, DH), BF16), vm(per + (NZ, chunk, DH), BF16)]
        + [vm(per + (NY, chunk, DH), BF16)] * 2
        + [vm(per + (NX, DH, DH), BF16)] * 4
        + [pltpu.SemaphoreType.DMA(per + (7,))] * 2
        + [pltpu.SemaphoreType.DMA((8,))]
    )
    out = jax.ShapeDtypeStruct(full, BF16)
    return pl.pallas_call(
        kernel,
        out_shape=(out,) * 4,
        in_specs=[pl.BlockSpec(memory_space=pl.ANY)] * 4,
        out_specs=(pl.BlockSpec(memory_space=pl.ANY),) * 4,
        scratch_shapes=scratch,
        compiler_params=pltpu.CompilerParams(
            collective_id=0, has_side_effects=True, vmem_limit_bytes=48 * 1024 * 1024
        ),
        cost_estimate=pl.CostEstimate(
            flops=24 * heads * rows * DH * DH, bytes_accessed=16 * rows * feats,
            transcendentals=rows * heads,
        ),
    )(queries, key_rows, value_rows, grad_output)


def solution(mesh):
    spec = P(("context", "tensor"), None)
    return jax.shard_map(
        body, mesh=mesh, in_specs=(spec,) * 4, out_specs=(spec,) * 4, check_vma=False
    )
```

time: 269 us -> 77.1 us (0.29)
  waiting for transfers between devices: 148 us -> 0 us
  Pallas kernels: 0 us -> 68.8 us
  starting transfers between devices: 53.5 us -> 0 us
  other arithmetic: 14.1 us -> 0 us
  between operations: 14 us -> 0.65 us
  blocking collectives: 12.6 us -> 0 us
  matrix products: 11.3 us -> 0 us
  local copies, waits for them, and re-layouts: 14.8 us -> 7.33 us
    all_gather x4 -> x0, waiting for transfers between devices: 113 us -> none  [entering(): pieces = lax.all_gather(running, axis)]
    pallas_call x0 -> x1, Pallas kernels: none -> 68.8 us  [body(): pl.pallas_call(kernel, out_shape=(out,) * 4, in_specs=[pl.BlockSpec(memor...]
    all_to_all x7 -> x0, starting transfers between devices: 53.4 us -> none  [the longest x1 10.4 us: body(): lax.all_to_all(key_rows, 'tensor', split_axis=1, concat_axis=0, tiled=True)]
    all_to_all x7 -> x0, waiting for transfers between devices: 34.9 us -> none  [the longest x1 9.22 us: body(): lax.all_to_all(key_rows, 'tensor', split_axis=1, concat_axis=0, tiled=True)]
    all_to_all x1 -> x0, blocking collectives: 12.6 us -> none  [body(): lax.all_to_all(value_rows, 'tensor', split_axis=1, concat_axis=0, tiled=T...]
    dot_general x12 -> x0, matrix products: 11.3 us -> none  [the longest x2 1.62 us: block_sums(): jnp.einsum('sjhd,sjhe->shde', left, right, preferred_element_type=jnp.flo...]
    add x5 -> x0, other arithmetic: 8.32 us -> none  [the longest x2 4.03 us: add_states(): return earlier + later]
    all_to_all x6 -> x0, local copies, waits for them, and re-layouts: 7.36 us -> none  [the longest x1 2.04 us: body(): lax.all_to_all(grad_value, 'tensor', split_axis=0, concat_axis=1, tiled=T...]
  transfers between devices with their start and end apart: 11 -> 0, of which waited for: 9 -> 0; matrix products, arithmetic and copies ran while one was open for 10% -> 0% of each run, Pallas kernels for 0% -> 0%
where the time goes in v1:
time: 77.1 us; the launch traced here: 76.8 us
  Pallas kernels  68.8 us (89%)
  local copies, waits for them, and re-layouts  7.33 us (10%)
    pallas_call x1, Pallas kernels, body(): pl.pallas_call(kernel, out_shape=(out,) * 4, in_specs=[pl.BlockSpec(memor...  68.8 us
    unnamed x12, local copies, waits for them, and re-layouts  7.33 us

profile of v1, /device:TPU:1, one launch (start us, length us, event | category | flops | bytes accessed | tf_op | source)
XLA Modules:
  0.0 76.8 jit_solution(7531081412418973856)
XLA Ops:
  0.6 0.0 copy-start
  0.6 1.0 %copy-done = bf16[128,2048]{1,0:T(8,128)(2,1)S(1)} copy-done((bf16[128,2048]{1,0:T(8,128)(2,1)S(1)}, bf16[128,2048]{1,0:T(8,128)(2,1)}, u32[]{:S(2)}) %copy-start) | copy-done | bytes 524312
  1.7 0.0 copy-start.1
  1.7 1.0 %copy-done.1 = bf16[128,2048]{1,0:T(8,128)(2,1)S(1)} copy-done((bf16[128,2048]{1,0:T(8,128)(2,1)S(1)}, bf16[128,2048]{1,0:T(8,128)(2,1)}, u32[]{:S(2)}) %copy-start.1) | copy-done | bytes 524312
  2.7 0.0 copy-start.2
  2.7 1.0 %copy-done.2 = bf16[128,2048]{1,0:T(8,128)(2,1)S(1)} copy-done((bf16[128,2048]{1,0:T(8,128)(2,1)S(1)}, bf16[128,2048]{1,0:T(8,128)(2,1)}, u32[]{:S(2)}) %copy-start.2) | copy-done | bytes 524312
  3.8 0.0 copy-start.3
  3.8 1.0 %copy-done.3 = bf16[128,2048]{1,0:T(8,128)(2,1)S(1)} copy-done((bf16[128,2048]{1,0:T(8,128)(2,1)S(1)}, bf16[128,2048]{1,0:T(8,128)(2,1)}, u32[]{:S(2)}) %copy-start.3) | copy-done | bytes 524312
  4.8 68.8 %shard_map.75 = (bf16[128,2048]{1,0:T(8,128)(2,1)S(1)}, bf16[128,2048]{1,0:T(8,128)(2,1)S(1)}, bf16[128,2048]{1,0:T(8,128)(2,1)S(1)}, bf16[128,2048]{1,0:T(8,128)(2,1)S(1)}) custom-call(bf16[128,2048]{1,0:T(8,128)(2,1)S(1)} %copy-done, bf16[128,2048]{1,0:T(8,128)(2,1)S(1)} %copy-done.1, bf16[128,2048]{1,0:T(8,128)(2,1)S(1)} %copy-done.2, ...), custom_call_target="tpu_custom_call" | custom-call | flops 805306368 | bytes 4194304 | tf_op jit(solution)/shard_map/pallas_call | solution.py:301
  73.6 0.8 %copy.12 = bf16[128,2048]{1,0:T(8,128)(2,1)} copy(bf16[128,2048]{1,0:T(8,128)(2,1)S(1)} %get-tuple-element.8) | data formatting | bytes 1048576
  74.4 0.8 %copy.13 = bf16[128,2048]{1,0:T(8,128)(2,1)} copy(bf16[128,2048]{1,0:T(8,128)(2,1)S(1)} %get-tuple-element.9) | data formatting | bytes 1048576
  75.2 0.8 %copy.14 = bf16[128,2048]{1,0:T(8,128)(2,1)} copy(bf16[128,2048]{1,0:T(8,128)(2,1)S(1)} %get-tuple-element.10) | data formatting | bytes 1048576
  76.0 0.8 %copy.15 = bf16[128,2048]{1,0:T(8,128)(2,1)} copy(bf16[128,2048]{1,0:T(8,128)(2,1)S(1)} %get-tuple-element.11) | data formatting | bytes 1048576
Async XLA Ops:
  0.6 1.0 %copy-start = (bf16[128,2048]{1,0:T(8,128)(2,1)S(1)}, bf16[128,2048]{1,0:T(8,128)(2,1)}, u32[]{:S(2)}) copy-start(bf16[128,2048]{1,0:T(8,128)(2,1)} %q_in.1) | copy-start | bytes 1572868
  1.7 1.0 %copy-start.1 = (bf16[128,2048]{1,0:T(8,128)(2,1)S(1)}, bf16[128,2048]{1,0:T(8,128)(2,1)}, u32[]{:S(2)}) copy-start(bf16[128,2048]{1,0:T(8,128)(2,1)} %k_in.1) | copy-start | bytes 1572868
  2.7 1.0 %copy-start.2 = (bf16[128,2048]{1,0:T(8,128)(2,1)S(1)}, bf16[128,2048]{1,0:T(8,128)(2,1)}, u32[]{:S(2)}) copy-start(bf16[128,2048]{1,0:T(8,128)(2,1)} %v_in.1) | copy-start | bytes 1572868
  3.8 1.0 %copy-start.3 = (bf16[128,2048]{1,0:T(8,128)(2,1)S(1)}, bf16[128,2048]{1,0:T(8,128)(2,1)}, u32[]{:S(2)}) copy-start(bf16[128,2048]{1,0:T(8,128)(2,1)} %g_in.1) | copy-start | bytes 1572868

commit v2 on v1

--- a/solution.py
+++ b/solution.py
@@ -42,19 +42,28 @@
     def at_z(i):
         return (i * NY + y, ten)
 
+    half = q.shape[1] // NC
+
+    def side(core):
+        return pl.ds(pl.multiple_of(core * half, half), half)
+
+    loads = []
+    for core in (peer, c):
+        for src, dst in ((k_in, k), (v_in, v)):
+            loads.append((src.at[:, side(core)], dst.at[:, side(core)]))
+    loads += [(q_in, q), (g_in, g)]
+    loads = [pltpu.make_async_copy(*pair, io_sem.at[i]) for i, pair in enumerate(loads)]
+    for load in loads:
+        load.start()
+
     rings = ((at_x, x, NX), (at_y, y, NY), (at_z, z, NZ))
     barrier = pltpu.get_barrier_semaphore()
-    pl.semaphore_signal(barrier, inc=1, device_id=at_core(), device_id_type=MESH)
-    for place, me, n in rings:
-        for off in range(1, n):
+    for place, me, n in rings[::-1]:
+        for off in sorted(range(1, n), key=lambda step: abs(step - n // 2)):
             pl.semaphore_signal(
                 barrier, inc=1, device_id=place(lax.rem(me + off, n)), device_id_type=MESH
             )
-
-    loads = []
-    for i, (src, dst) in enumerate(((k_in, k), (v_in, v), (q_in, q), (g_in, g))):
-        loads.append(pltpu.make_async_copy(src, dst, io_sem.at[i]))
-        loads[-1].start()
+    pl.semaphore_signal(barrier, inc=1, device_id=at_core(), device_id_type=MESH)
 
     row_id = lax.broadcasted_iota(jnp.int32, (rows, rows), 0)
     col_id = lax.broadcasted_iota(jnp.int32, (rows, rows), 1)
@@ -87,11 +96,6 @@
         pending.append(all_of)
         return all_of
 
-    def settle():
-        for p in pending:
-            p().wait_send()
-        pending.clear()
-
     waits = {}
 
     def term(d, h):
@@ -102,7 +106,6 @@
     def core_up(d, s):
         for i in range(NX):
             cu_s[d, s, i] = term(d, head(peer, i, s)).astype(BF16)
-        return lambda: None
 
     def core_up_send(d, s):
         def whole():
@@ -111,6 +114,8 @@
         whole().start()
         pending.append(whole)
         waits[d, s, 0] = whole
+
+    def own_terms(d, s):
         for i in range(NX):
             mine[d, s, i] = term(d, head(c, i, s))
 
@@ -126,23 +131,25 @@
 
     def y_up(d, s):
         waits[d, s, 1]().wait_recv()
+        terms = [xu_r[d, s, i].astype(F32) for i in range(NX)]
+        yu_s[d, s] = sum(terms[1:], terms[0]).astype(BF16).reshape(NY, DH // NY, DH)
+        waits[d, s, 2] = scatter(yu_s.at[d, s], yu_r.at[d, s], d, s, 2, 1)
+        yu_r[d, s, y] = yu_s[d, s, y]
         run = jnp.zeros((DH, DH), F32)
         for i in order(d, NX):
             xpre[d, s, i] = run
             run = run + xu_r[d, s, i].astype(F32)
-        yu_s[d, s] = run.astype(BF16).reshape(NY, DH // NY, DH)
-        waits[d, s, 2] = scatter(yu_s.at[d, s], yu_r.at[d, s], d, s, 2, 1)
-        yu_r[d, s, y] = yu_s[d, s, y]
 
     def z_all(d, s):
         waits[d, s, 2]().wait_recv()
+        terms = [yu_r[d, s, i].astype(F32) for i in range(NY)]
+        z_s[d, s] = sum(terms[1:], terms[0]).astype(z_s.dtype)
+        waits[d, s, 3] = scatter(z_s.at[d, s], z_r.at[d, s], d, s, 3, 2, whole=True)
+        z_r[d, s, z] = z_s[d, s]
         run = jnp.zeros((DH // NY, DH), F32)
         for i in order(d, NY):
             ypre[d, s, i] = run
             run = run + yu_r[d, s, i].astype(F32)
-        z_s[d, s] = run.astype(z_s.dtype)
-        waits[d, s, 3] = scatter(z_s.at[d, s], z_r.at[d, s], d, s, 3, 2, whole=True)
-        z_r[d, s, z] = z_s[d, s]
 
     def y_down(d, s):
         waits[d, s, 3]().wait_recv()
@@ -165,18 +172,26 @@
 
     def core_down(d, s):
         waits[d, s, 5]().wait_recv()
-        first = 0 if d == 0 else 1
-        for i in range(NX):
-            chip = xd_r[d, s, i].astype(F32)
-            cd_s[d, s, i] = (chip + jnp.where(c == first, mine[d, s, i], 0.0)).astype(BF16)
-            own_pre[d, s, i] = (
-                chip + jnp.where(c == first, 0.0, cu_r[d, s, i].astype(F32))
-            ).astype(BF16)
-
-        def whole():
-            return copy(cd_s.at[d, s], cd_r.at[d, s], d, s, 6, at_core())
-
-        whole().start()
+        adds_mine = c == (0 if d == 0 else 1)
+
+        def whole(src=cd_s):
+            return copy(src.at[d, s], cd_r.at[d, s], d, s, 6, at_core())
+
+        @pl.when(adds_mine)
+        def _():
+            for i in range(NX):
+                cd_s[d, s, i] = (xd_r[d, s, i].astype(F32) + mine[d, s, i]).astype(BF16)
+            whole().start()
+            own_pre[d, s] = xd_r[d, s]
+
+        @pl.when(jnp.logical_not(adds_mine))
+        def _():
+            whole(xd_r).start()
+            for i in range(NX):
+                own_pre[d, s, i] = (
+                    xd_r[d, s, i].astype(F32) + cu_r[d, s, i].astype(F32)
+                ).astype(BF16)
+
         pending.append(whole)
         waits[d, s, 6] = whole
 
@@ -222,27 +237,32 @@
 
     loads[0].wait()
     loads[1].wait()
-    for s in streams:
-        core_up(0, s)
-        if s == 0:
-            pl.semaphore_wait(barrier, 1 + (NX - 1) + (NY - 1) + (NZ - 1))
-        core_up_send(0, s)
+    core_up(0, 0)
+    pl.semaphore_wait(barrier, 1 + (NX - 1) + (NY - 1) + (NZ - 1))
+    core_up_send(0, 0)
+    core_up(0, 1)
+    core_up_send(0, 1)
     loads[2].wait()
     loads[3].wait()
+    for s in streams:
+        own_terms(0, s)
+    loads[4].wait()
+    loads[5].wait()
     work = [(core, s) for s in streams for core in (c, peer)]
     for j, stage in enumerate(middle):
         for s in streams:
             stage(0, s)
         if j < len(work):
             local_forward(*work[j])
-    settle()
+    sent = list(pending)
     for s in streams:
         normalize(c, s, own_pre)
         waits[0, s, 6]().wait_recv()
         normalize(peer, s, cd_r)
         core_up(1, s)
         core_up_send(1, s)
-    att_copy = pltpu.make_async_copy(att, att_out, io_sem.at[4])
+        own_terms(1, s)
+    att_copy = pltpu.make_async_copy(att, att_out, io_sem.at[6])
     att_copy.start()
     for j, stage in enumerate(middle):
         for s in streams:
@@ -251,22 +271,44 @@
             core, s = work[j]
             local_backward(core, s, own_pre if core is c else cd_r)
         if j + 1 == len(work):
-            gq_copy = pltpu.make_async_copy(gq, gq_out, io_sem.at[5])
+            gq_copy = pltpu.make_async_copy(gq, gq_out, io_sem.at[7])
             gq_copy.start()
-    settle_later = list(pending)
+            for one in sent:
+                one().wait_send()
+                pending.remove(one)
+
+    last = []
+
+    def leave(core, at):
+        for i, (src, dst) in enumerate(((gk, gk_out), (gv, gv_out))):
+            move = pltpu.make_async_copy(
+                src.at[:, side(core)], dst.at[:, side(core)], io_sem.at[at + i]
+            )
+            move.start()
+            last.append(move)
+
     for s in streams:
         finish(c, s, own_pre)
+    leave(c, 8)
+    for s in streams:
         waits[1, s, 6]().wait_recv()
         finish(peer, s, cd_r)
-    gk_copy = pltpu.make_async_copy(gk, gk_out, io_sem.at[6])
-    gv_copy = pltpu.make_async_copy(gv, gv_out, io_sem.at[7])
-    gk_copy.start()
-    gv_copy.start()
-    settle()
-    att_copy.wait()
-    gq_copy.wait()
-    gk_copy.wait()
-    gv_copy.wait()
+    leave(peer, 10)
+    for one in pending:
+        one().wait_send()
+    for move in [att_copy, gq_copy] + last:
+        move.wait()
+
+
+def hand_over(a, b, c, d, a_out, b_out, c_out, d_out, sem):
+    copies = [
+        pltpu.make_async_copy(src, dst, sem.at[i])
+        for i, (src, dst) in enumerate(((a, a_out), (b, b_out), (c, c_out), (d, d_out)))
+    ]
+    for move in copies:
+        move.start()
+    for move in copies:
+        move.wait()
 
 
 def body(queries, key_rows, value_rows, grad_output):
@@ -295,23 +337,31 @@
         + [vm(per + (NY, chunk, DH), BF16)] * 2
         + [vm(per + (NX, DH, DH), BF16)] * 4
         + [pltpu.SemaphoreType.DMA(per + (7,))] * 2
-        + [pltpu.SemaphoreType.DMA((8,))]
+        + [pltpu.SemaphoreType.DMA((12,))]
     )
     out = jax.ShapeDtypeStruct(full, BF16)
-    return pl.pallas_call(
+    results = pl.pallas_call(
         kernel,
         out_shape=(out,) * 4,
-        in_specs=[pl.BlockSpec(memory_space=pl.ANY)] * 4,
+        in_specs=[pl.BlockSpec(memory_space=pltpu.HBM)] * 4,
         out_specs=(pl.BlockSpec(memory_space=pl.ANY),) * 4,
         scratch_shapes=scratch,
         compiler_params=pltpu.CompilerParams(
-            collective_id=0, has_side_effects=True, vmem_limit_bytes=48 * 1024 * 1024
+            collective_id=0, has_side_effects=True, vmem_limit_bytes=52864 * 1024
         ),
         cost_estimate=pl.CostEstimate(
             flops=24 * heads * rows * DH * DH, bytes_accessed=16 * rows * feats,
             transcendentals=rows * heads,
         ),
     )(queries, key_rows, value_rows, grad_output)
+    return pl.pallas_call(
+        hand_over,
+        out_shape=(out,) * 4,
+        in_specs=[pl.BlockSpec(memory_space=pl.ANY)] * 4,
+        out_specs=(pl.BlockSpec(memory_space=pl.ANY),) * 4,
+        scratch_shapes=[pltpu.SemaphoreType.DMA((4,))],
+        compiler_params=pltpu.CompilerParams(vmem_limit_bytes=8 * 1024 * 1024),
+    )(*results)
 
 
 def solution(mesh):

time: 77.1 us -> 69.8 us (0.905)
  local copies, waits for them, and re-layouts: 7.33 us -> 0 us
    unnamed x12 -> x0, local copies, waits for them, and re-layouts: 7.33 us -> none
    pallas_call x0 -> x1, Pallas kernels: none -> 1.35 us  [body(): pl.pallas_call(hand_over, out_shape=(out,) * 4, in_specs=[pl.BlockSpec(me...]
    pallas_call x1, Pallas kernels: 68.8 us -> 67.7 us  [body(): pl.pallas_call(kernel, out_shape=(out,) * 4, in_specs=[pl.BlockSpec(memor...]
where the time goes in v2:
time: 69.8 us; the launch traced here: 69.7 us
  Pallas kernels  69.1 us (99%)
    pallas_call x1, Pallas kernels, body(): pl.pallas_call(kernel, out_shape=(out,) * 4, in_specs=[pl.BlockSpec(memor...  67.7 us

profile of v2, /device:TPU:1, one launch (start us, length us, event | category | flops | bytes accessed | tf_op | source)
XLA Modules:
  0.0 69.7 jit_solution(2448401273517114000)
XLA Ops:
  0.6 67.7 %shard_map.75 = (bf16[128,2048]{1,0:T(8,128)(2,1)S(1)}, bf16[128,2048]{1,0:T(8,128)(2,1)S(1)}, bf16[128,2048]{1,0:T(8,128)(2,1)S(1)}, bf16[128,2048]{1,0:T(8,128)(2,1)S(1)}) custom-call(bf16[128,2048]{1,0:T(8,128)(2,1)} %q_in.1, bf16[128,2048]{1,0:T(8,128)(2,1)} %k_in.1, bf16[128,2048]{1,0:T(8,128)(2,1)} %v_in.1, bf16[128,2048]{1,0:T(8,128)(2,1)} %g_in.1), custom_call_target="tpu_custom_call" | custom-call | flops 805306368 | bytes 4194304 | tf_op jit(solution)/shard_map/pallas_call | solution.py:343
  68.3 1.3 %shard_map.76 = (bf16[128,2048]{1,0:T(8,128)(2,1)}, bf16[128,2048]{1,0:T(8,128)(2,1)}, bf16[128,2048]{1,0:T(8,128)(2,1)}, bf16[128,2048]{1,0:T(8,128)(2,1)}) custom-call(bf16[128,2048]{1,0:T(8,128)(2,1)S(1)} %get-tuple-element.8.a, bf16[128,2048]{1,0:T(8,128)(2,1)S(1)} %get-tuple-element.9.b, bf16[128,2048]{1,0:T(8,128)(2,1)S(1)} %get-tuple-element.10.c, ...), custom_call_target="tpu_custom_call" | custom-call | tf_op jit(solution)/shard_map/pallas_call | solution.py:357

commit v3 on v2

v3 whole, which is shorter than its diff:
```python
import jax
import jax.numpy as jnp
from jax import lax
from jax.experimental import pallas as pl
from jax.experimental.pallas import tpu as pltpu
from jax.sharding import PartitionSpec as P

DH = 128
NZ, NY, NX, NC = 8, 8, 4, 2
STREAMS = 2
EPS = 1e-06
MESH = pl.DeviceIdType.MESH
F32 = jnp.float32
BF16 = jnp.bfloat16


def dot(a, b, ca, cb):
    return lax.dot_general(a, b, (((ca,), (cb,)), ((), ())), preferred_element_type=F32)


def kernel(
    q_in, k_in, v_in, g_in, att_out, gq_out, gk_out, gv_out,
    q, k, v, g, w, local, da, att, gq, gk, gv, gkl, gvl,
    first_term, second_state, xu_s, xu_r, xpre, yu_s, yu_r, ypre, z_s, z_r,
    yd_s, yd_r, xd_s, xd_r, ssem, rsem, own_sem, far_s, far_r,
):
    rows, half = q.shape[1], q.shape[2]
    part = half // STREAMS
    ctx, ten = lax.axis_index("context"), lax.axis_index("tensor")
    z, y = ctx // NY, lax.rem(ctx, NY)
    x, c = ten // NC, lax.rem(ten, NC)
    peer = 1 - c
    to_peer = (ctx, x * NC + peer)
    streams = range(STREAMS)

    def at_x(i):
        return (ctx, i * NC + c)

    def at_y(i):
        return (z * NY + i, ten)

    def at_z(i):
        return (i * NY + y, ten)

    def span(core, s):
        if s is None:
            return pl.ds(pl.multiple_of(core * half, half), half)
        return pl.ds(pl.multiple_of(core * half + s * part, part), part)

    def within(s):
        return pl.ds(0, half) if s is None else pl.ds(s * part, part)

    def near(i, src, dst):
        return pltpu.make_async_copy(src, dst, own_sem.at[i])

    def far(i, src, dst):
        return pltpu.make_async_remote_copy(
            src_ref=src, dst_ref=dst, send_sem=far_s.at[i], recv_sem=far_r.at[i],
            device_id=to_peer, device_id_type=MESH,
        )

    entering = [(k_in, k, 0), (v_in, v, 0), (k_in, k, 1), (v_in, v, 1), (q_in, q, None), (g_in, g, None)]
    own_in = [
        near(i, src.at[:, span(c, s)], dst.at[c, :, within(s)])
        for i, (src, dst, s) in enumerate(entering)
    ]
    far_in = [
        far(i, src.at[:, span(peer, s)], dst.at[c, :, within(s)])
        for i, (src, dst, s) in enumerate(entering)
    ]
    for move in own_in:
        move.start()

    rings = ((at_x, x, NX), (at_y, y, NY), (at_z, z, NZ))
    barrier = pltpu.get_barrier_semaphore()
    pl.semaphore_signal(barrier, inc=1, device_id=to_peer, device_id_type=MESH)
    for place, me, n in rings[::-1]:
        for off in sorted(range(1, n), key=lambda step: abs(step - n // 2)):
            pl.semaphore_signal(
                barrier, inc=1, device_id=place(lax.rem(me + off, n)), device_id_type=MESH
            )

    row_id = lax.broadcasted_iota(jnp.int32, (rows, rows), 0)
    col_id = lax.broadcasted_iota(jnp.int32, (rows, rows), 1)
    causal = row_id >= col_id

    def cols(h):
        return pl.ds(pl.multiple_of(h * DH, DH), DH)

    def copy(src, dst, d, s, r, to):
        return pltpu.make_async_remote_copy(
            src_ref=src, dst_ref=dst, send_sem=ssem.at[d, s, r], recv_sem=rsem.at[d, s, r],
            device_id=to, device_id_type=MESH,
        )

    pending = []
    waits = {}

    def expect(dst, d, s, r, ring):
        place, me, n = rings[ring]

        def all_of():
            slots = dst.at[pl.ds(0, n - 1)]
            return copy(slots, slots, d, s, r, place(lax.rem(me + 1, n)))

        pending.append(all_of)
        waits[d, s, r] = all_of

    def scatter(src, dst, d, s, r, ring, whole=False):
        place, me, n = rings[ring]
        for off in range(1, n):
            to = lax.rem(me + off, n)
            copy(src if whole else src.at[to], dst.at[me], d, s, r, place(to)).start()
        expect(dst, d, s, r, ring)

    def order(d, n):
        return range(n) if d == 0 else range(n - 1, -1, -1)

    def x_up(d, s):
        left, right = (k, v) if d == 0 else (q, da)
        for off in list(range(1, NX)) + [0]:
            i = lax.rem(x + off, NX)
            at = cols(s * NX + i)
            ones = [dot(left[b, :, at], right[b, :, at], 0, 0) for b in order(d, NC)]
            total = (ones[0] + ones[1]).astype(BF16)
            if off:
                xu_s[d, s, i] = total
                copy(xu_s.at[d, s, i], xu_r.at[d, s, x], d, s, 0, at_x(i)).start()
            else:
                xu_r[d, s, x] = total
            first_term[d, s, i] = ones[0]
        expect(xu_r.at[d, s], d, s, 0, 0)

    def y_up(d, s):
        waits[d, s, 0]().wait_recv()
        terms = [xu_r[d, s, i].astype(F32) for i in range(NX)]
        yu_s[d, s] = sum(terms[1:], terms[0]).astype(BF16).reshape(NY, DH // NY, DH)
        scatter(yu_s.at[d, s], yu_r.at[d, s], d, s, 1, 1)
        yu_r[d, s, y] = yu_s[d, s, y]
        run = jnp.zeros((DH, DH), F32)
        for i in order(d, NX):
            xpre[d, s, i] = run
            run = run + xu_r[d, s, i].astype(F32)

    def z_all(d, s):
        waits[d, s, 1]().wait_recv()
        terms = [yu_r[d, s, i].astype(F32) for i in range(NY)]
        z_s[d, s] = sum(terms[1:], terms[0]).astype(z_s.dtype)
        scatter(z_s.at[d, s], z_r.at[d, s], d, s, 2, 2, whole=True)
        z_r[d, s, z] = z_s[d, s]
        run = jnp.zeros((DH // NY, DH), F32)
        for i in order(d, NY):
            ypre[d, s, i] = run
            run = run + yu_r[d, s, i].astype(F32)

    def y_down(d, s):
        waits[d, s, 2]().wait_recv()
        base = jnp.zeros((DH // NY, DH), F32)
        for i in range(NZ):
            passed = i < z if d == 0 else i > z
            base = base + jnp.where(passed, z_r[d, s, i].astype(F32), 0.0)
        for i in range(NY):
            yd_s[d, s, i] = (base + ypre[d, s, i]).astype(BF16)
        scatter(yd_s.at[d, s], yd_r.at[d, s], d, s, 3, 1)
        yd_r[d, s, y] = yd_s[d, s, y]

    def x_down(d, s):
        waits[d, s, 3]().wait_recv()
        base = yd_r[d, s].reshape(DH, DH).astype(F32)
        for i in range(NX):
            xd_s[d, s, i] = (base + xpre[d, s, i]).astype(BF16)
        scatter(xd_s.at[d, s], xd_r.at[d, s], d, s, 4, 0)
        xd_r[d, s, x] = xd_s[d, s, x]

    def arrive(d, s):
        waits[d, s, 4]().wait_recv()
        for i in range(NX):
            second_state[d, s, i] = (xd_r[d, s, i].astype(F32) + first_term[d, s, i]).astype(BF16)

    def state(d, s, b, i):
        return xd_r[d, s, i] if b == order(d, NC)[0] else second_state[d, s, i]

    def local_forward(s, b):
        for i in range(NX):
            h = s * NX + i
            at = cols(h)
            sc = dot(q[b, :, at], k[b, :, at], 1, 1)
            wt = jnp.where(causal, sc, 0.0).astype(BF16)
            w[b, h] = wt
            local[b, :, at] = dot(wt, v[b, :, at], 1, 0)

    def normalize(s, b):
        for i in range(NX):
            at = cols(s * NX + i)
            a = local[b, :, at] + dot(q[b, :, at], state(0, s, b, i), 1, 0)
            inv = lax.rsqrt(jnp.mean(a * a, axis=-1, keepdims=True) + EPS)
            normed = a * inv
            att[b, :, at] = normed.astype(BF16)
            cot = g[b, :, at].astype(F32)
            m = jnp.mean(cot * normed, axis=-1, keepdims=True)
            da[b, :, at] = ((cot - normed * m) * inv).astype(BF16)

    def local_backward(s, b):
        for i in range(NX):
            h = s * NX + i
            at = cols(h)
            d_a = da[b, :, at]
            dw = jnp.where(causal, dot(d_a, v[b, :, at], 1, 1), 0.0).astype(BF16)
            gq[b, :, at] = (
                dot(dw, k[b, :, at], 1, 0) + dot(d_a, state(0, s, b, i), 1, 1)
            ).astype(BF16)
            gkl[b, :, at] = dot(dw, q[b, :, at], 0, 0)
            gvl[b, :, at] = dot(w[b, h], d_a, 0, 0)

    def finish(s, b):
        for i in range(NX):
            at = cols(s * NX + i)
            suf = state(1, s, b, i)
            gk[b, :, at] = (gkl[b, :, at] + dot(v[b, :, at], suf, 1, 1)).astype(BF16)
            gv[b, :, at] = (gvl[b, :, at] + dot(k[b, :, at], suf, 1, 0)).astype(BF16)

    leaving = []

    def leave(i, src, dst, s):
        pair = (
            far(i, src.at[peer, :, within(s)], dst.at[:, span(c, s)]),
            near(i, src.at[c, :, within(s)], dst.at[:, span(c, s)]),
        )
        for move in pair:
            move.start()
        leaving.append(pair)

    pl.semaphore_wait(barrier, 1 + (NX - 1) + (NY - 1) + (NZ - 1))
    for move in far_in:
        move.start()

    def ready(*which):
        for i in which:
            own_in[i].wait()
            far_in[i].wait_recv()

    ready(0, 1)
    x_up(0, 0)
    ready(2, 3)
    x_up(0, 1)
    ready(4, 5)
    middle = (y_up, z_all, y_down, x_down)
    work = [(s, b) for s in streams for b in range(NC)]
    local_forward(*work[0])
    for j, stage in enumerate(middle):
        for s in streams:
            stage(0, s)
        if j + 1 < len(work):
            local_forward(*work[j + 1])
    sent = list(pending)
    for s in streams:
        arrive(0, s)
        for b in range(NC):
            normalize(s, b)
        x_up(1, s)
    leave(6, att, att_out, None)
    local_backward(*work[0])
    for j, stage in enumerate(middle):
        for s in streams:
            stage(1, s)
        if j + 1 < len(work):
            local_backward(*work[j + 1])
    leave(7, gq, gq_out, None)
    for one in sent:
        one().wait_send()
        pending.remove(one)
    for move in far_in:
        move.wait_send()
    for s in streams:
        arrive(1, s)
        for b in range(NC):
            finish(s, b)
        leave(8 + 2 * s, gk, gk_out, s)
        leave(9 + 2 * s, gv, gv_out, s)
    for one in pending:
        one().wait_send()
    for away, home in leaving:
        home.wait()
        away.wait_send()
        away.wait_recv()


def hand_over(a, b, c, d, a_out, b_out, c_out, d_out, sem):
    copies = [
        pltpu.make_async_copy(src, dst, sem.at[i])
        for i, (src, dst) in enumerate(((a, a_out), (b, b_out), (c, c_out), (d, d_out)))
    ]
    for move in copies:
        move.start()
    for move in copies:
        move.wait()


def body(queries, key_rows, value_rows, grad_output):
    rows, feats = queries.shape
    half = feats // NC
    heads = half // DH
    per = (2, STREAMS)
    both = (NC, rows, half)
    chunk = DH // NY

    def vm(shape, dtype):
        return pltpu.VMEM(shape, dtype)

    square, strip = per + (NX, DH, DH), per + (NY, chunk, DH)
    scratch = (
        [vm(both, BF16)] * 4
        + [vm((NC, heads, rows, rows), BF16), vm(both, F32), vm(both, BF16)]
        + [vm(both, BF16)] * 4
        + [vm(both, F32)] * 2
        + [vm(square, F32), vm(square, BF16)]
        + [vm(square, BF16)] * 2
        + [vm(square, F32)]
        + [vm(strip, BF16)] * 2
        + [vm(strip, F32)]
        + [vm(per + (chunk, DH), BF16), vm(per + (NZ, chunk, DH), BF16)]
        + [vm(strip, BF16)] * 2
        + [vm(square, BF16)] * 2
        + [pltpu.SemaphoreType.DMA(per + (5,))] * 2
        + [pltpu.SemaphoreType.DMA((12,))] * 3
    )
    out = jax.ShapeDtypeStruct((rows, feats), BF16)
    results = pl.pallas_call(
        kernel,
        out_shape=(out,) * 4,
        in_specs=[pl.BlockSpec(memory_space=pltpu.HBM)] * 4,
        out_specs=(pl.BlockSpec(memory_space=pl.ANY),) * 4,
        scratch_shapes=scratch,
        compiler_params=pltpu.CompilerParams(
            collective_id=0, has_side_effects=True, vmem_limit_bytes=52864 * 1024
        ),
        cost_estimate=pl.CostEstimate(
            flops=24 * NC * heads * rows * DH * DH, bytes_accessed=16 * rows * feats,
            transcendentals=rows * NC * heads,
        ),
    )(queries, key_rows, value_rows, grad_output)
    return pl.pallas_call(
        hand_over,
        out_shape=(out,) * 4,
        in_specs=[pl.BlockSpec(memory_space=pl.ANY)] * 4,
        out_specs=(pl.BlockSpec(memory_space=pl.ANY),) * 4,
        scratch_shapes=[pltpu.SemaphoreType.DMA((4,))],
        compiler_params=pltpu.CompilerParams(vmem_limit_bytes=8 * 1024 * 1024),
    )(*results)


def solution(mesh):
    spec = P(("context", "tensor"), None)
    return jax.shard_map(
        body, mesh=mesh, in_specs=(spec,) * 4, out_specs=(spec,) * 4, check_vma=False
    )
```

time: 69.8 us -> 68.1 us (0.976)
  Pallas kernels: 69.1 us -> 67.4 us
    pallas_call x1, Pallas kernels: 67.7 us -> 66 us  [body(): pl.pallas_call(kernel, out_shape=(out,) * 4, in_specs=[pl.BlockSpec(memor...]
where the time goes in v3:
time: 68.1 us; the launch traced here: 68 us
  Pallas kernels  67.4 us (99%)
    pallas_call x1, Pallas kernels, body(): pl.pallas_call(kernel, out_shape=(out,) * 4, in_specs=[pl.BlockSpec(memor...  66 us

profile of v3, /device:TPU:1, one launch (start us, length us, event | category | flops | bytes accessed | tf_op | source)
XLA Modules:
  0.0 68.0 jit_solution(8700673461743138635)
XLA Ops:
  0.6 66.0 %shard_map.75 = (bf16[128,2048]{1,0:T(8,128)(2,1)S(1)}, bf16[128,2048]{1,0:T(8,128)(2,1)S(1)}, bf16[128,2048]{1,0:T(8,128)(2,1)S(1)}, bf16[128,2048]{1,0:T(8,128)(2,1)S(1)}) custom-call(bf16[128,2048]{1,0:T(8,128)(2,1)} %q_in.1, bf16[128,2048]{1,0:T(8,128)(2,1)} %k_in.1, bf16[128,2048]{1,0:T(8,128)(2,1)} %v_in.1, bf16[128,2048]{1,0:T(8,128)(2,1)} %g_in.1), custom_call_target="tpu_custom_call" | custom-call | flops 805306368 | bytes 4194304 | tf_op jit(solution)/shard_map/pallas_call | solution.py:328
  66.7 1.3 %shard_map.76 = (bf16[128,2048]{1,0:T(8,128)(2,1)}, bf16[128,2048]{1,0:T(8,128)(2,1)}, bf16[128,2048]{1,0:T(8,128)(2,1)}, bf16[128,2048]{1,0:T(8,128)(2,1)}) custom-call(bf16[128,2048]{1,0:T(8,128)(2,1)S(1)} %get-tuple-element.8.a, bf16[128,2048]{1,0:T(8,128)(2,1)S(1)} %get-tuple-element.9.b, bf16[128,2048]{1,0:T(8,128)(2,1)S(1)} %get-tuple-element.10.c, ...), custom_call_target="tpu_custom_call" | custom-call | tf_op jit(solution)/shard_map/pallas_call | solution.py:342

commit v4 on v3

--- a/solution.py
+++ b/solution.py
@@ -8,6 +8,7 @@
 DH = 128
 NZ, NY, NX, NC = 8, 8, 4, 2
 STREAMS = 2
+UNROLL = 1
 EPS = 1e-06
 MESH = pl.DeviceIdType.MESH
 F32 = jnp.float32
@@ -20,9 +21,8 @@
 
 def kernel(
     q_in, k_in, v_in, g_in, att_out, gq_out, gk_out, gv_out,
-    q, k, v, g, w, local, da, att, gq, gk, gv, gkl, gvl,
-    first_term, second_state, xu_s, xu_r, xpre, yu_s, yu_r, ypre, z_s, z_r,
-    yd_s, yd_r, xd_s, xd_r, ssem, rsem, own_sem, far_s, far_r,
+    q, k, v, g, w, qt, local, da, att, gq, gk, gv, gkl, gvl,
+    first_term, second_state, up_s, up_r, pre, z_s, z_r, down_s, down_r, ssem, rsem, own_sem, far_s, far_r,
 ):
     rows, half = q.shape[1], q.shape[2]
     part = half // STREAMS
@@ -33,11 +33,8 @@
     to_peer = (ctx, x * NC + peer)
     streams = range(STREAMS)
 
-    def at_x(i):
-        return (ctx, i * NC + c)
-
-    def at_y(i):
-        return (z * NY + i, ten)
+    def at_plane(i):
+        return (z * NY + i // NX, lax.rem(i, NX) * NC + c)
 
     def at_z(i):
         return (i * NY + y, ten)
@@ -71,11 +68,12 @@
     for move in own_in:
         move.start()
 
-    rings = ((at_x, x, NX), (at_y, y, NY), (at_z, z, NZ))
+    plane = NY * NX
+    rings = ((at_plane, y * NX + x, plane), (at_z, z, NZ))
     barrier = pltpu.get_barrier_semaphore()
     pl.semaphore_signal(barrier, inc=1, device_id=to_peer, device_id_type=MESH)
-    for place, me, n in rings[::-1]:
-        for off in sorted(range(1, n), key=lambda step: abs(step - n // 2)):
+    for place, me, n in rings:
+        for off in range(1, n):
             pl.semaphore_signal(
                 barrier, inc=1, device_id=place(lax.rem(me + off, n)), device_id_type=MESH
             )
@@ -108,77 +106,68 @@
 
     def scatter(src, dst, d, s, r, ring, whole=False):
         place, me, n = rings[ring]
-        for off in range(1, n):
+
+        def send(off, _):
             to = lax.rem(me + off, n)
             copy(src if whole else src.at[to], dst.at[me], d, s, r, place(to)).start()
+            return _
+
+        lax.fori_loop(1, n, send, 0, unroll=UNROLL)
         expect(dst, d, s, r, ring)
 
     def order(d, n):
         return range(n) if d == 0 else range(n - 1, -1, -1)
 
-    def x_up(d, s):
-        left, right = (k, v) if d == 0 else (q, da)
-        for off in list(range(1, NX)) + [0]:
-            i = lax.rem(x + off, NX)
-            at = cols(s * NX + i)
-            ones = [dot(left[b, :, at], right[b, :, at], 0, 0) for b in order(d, NC)]
+    def term(d, b, h):
+        if d == 0:
+            return dot(k[b, :, cols(h)], v[b, :, cols(h)], 0, 0)
+        return dot(qt[b, h], da[b, :, cols(h)], 1, 0)
+
+    here = y * NX + x
+
+    def up(d, s):
+        for i in range(NX):
+            ones = [term(d, b, s * NX + i) for b in order(d, NC)]
             total = (ones[0] + ones[1]).astype(BF16)
-            if off:
-                xu_s[d, s, i] = total
-                copy(xu_s.at[d, s, i], xu_r.at[d, s, x], d, s, 0, at_x(i)).start()
-            else:
-                xu_r[d, s, x] = total
+            up_s[d, s, i * NY : (i + 1) * NY] = total.reshape(NY, DH // NY, DH)
             first_term[d, s, i] = ones[0]
-        expect(xu_r.at[d, s], d, s, 0, 0)
-
-    def y_up(d, s):
+        scatter(up_s.at[d, s], up_r.at[d, s], d, s, 0, 0)
+        up_r[d, s, here] = up_s[d, s, here]
+
+    def z_all(d, s):
         waits[d, s, 0]().wait_recv()
-        terms = [xu_r[d, s, i].astype(F32) for i in range(NX)]
-        yu_s[d, s] = sum(terms[1:], terms[0]).astype(BF16).reshape(NY, DH // NY, DH)
-        scatter(yu_s.at[d, s], yu_r.at[d, s], d, s, 1, 1)
-        yu_r[d, s, y] = yu_s[d, s, y]
-        run = jnp.zeros((DH, DH), F32)
-        for i in order(d, NX):
-            xpre[d, s, i] = run
-            run = run + xu_r[d, s, i].astype(F32)
-
-    def z_all(d, s):
-        waits[d, s, 1]().wait_recv()
-        terms = [yu_r[d, s, i].astype(F32) for i in range(NY)]
-        z_s[d, s] = sum(terms[1:], terms[0]).astype(z_s.dtype)
-        scatter(z_s.at[d, s], z_r.at[d, s], d, s, 2, 2, whole=True)
+        total = up_r[d, s, 0].astype(F32)
+        for i in range(1, plane):
+            total = total + up_r[d, s, i].astype(F32)
+        z_s[d, s] = total.astype(BF16)
+        scatter(z_s.at[d, s], z_r.at[d, s], d, s, 1, 1, whole=True)
         z_r[d, s, z] = z_s[d, s]
         run = jnp.zeros((DH // NY, DH), F32)
-        for i in order(d, NY):
-            ypre[d, s, i] = run
-            run = run + yu_r[d, s, i].astype(F32)
-
-    def y_down(d, s):
-        waits[d, s, 2]().wait_recv()
+        for i in order(d, plane):
+            pre[d, s, i] = run
+            run = run + up_r[d, s, i].astype(F32)
+
+    def down(d, s):
+        waits[d, s, 1]().wait_recv()
         base = jnp.zeros((DH // NY, DH), F32)
         for i in range(NZ):
             passed = i < z if d == 0 else i > z
             base = base + jnp.where(passed, z_r[d, s, i].astype(F32), 0.0)
-        for i in range(NY):
-            yd_s[d, s, i] = (base + ypre[d, s, i]).astype(BF16)
-        scatter(yd_s.at[d, s], yd_r.at[d, s], d, s, 3, 1)
-        yd_r[d, s, y] = yd_s[d, s, y]
-
-    def x_down(d, s):
-        waits[d, s, 3]().wait_recv()
-        base = yd_r[d, s].reshape(DH, DH).astype(F32)
-        for i in range(NX):
-            xd_s[d, s, i] = (base + xpre[d, s, i]).astype(BF16)
-        scatter(xd_s.at[d, s], xd_r.at[d, s], d, s, 4, 0)
-        xd_r[d, s, x] = xd_s[d, s, x]
+        for i in range(plane):
+            down_s[d, s, i] = (base + pre[d, s, i]).astype(BF16)
+        scatter(down_s.at[d, s], down_r.at[d, s], d, s, 2, 0)
+        down_r[d, s, here] = down_s[d, s, here]
+
+    def arrived(d, s, i):
+        return down_r[d, s, i * NY : (i + 1) * NY].reshape(DH, DH)
 
     def arrive(d, s):
-        waits[d, s, 4]().wait_recv()
-        for i in range(NX):
-            second_state[d, s, i] = (xd_r[d, s, i].astype(F32) + first_term[d, s, i]).astype(BF16)
+        waits[d, s, 2]().wait_recv()
+        for i in range(NX):
+            second_state[d, s, i] = (arrived(d, s, i).astype(F32) + first_term[d, s, i]).astype(BF16)
 
     def state(d, s, b, i):
-        return xd_r[d, s, i] if b == order(d, NC)[0] else second_state[d, s, i]
+        return arrived(d, s, i) if b == order(d, NC)[0] else second_state[d, s, i]
 
     def local_forward(s, b):
         for i in range(NX):
@@ -187,6 +176,7 @@
             sc = dot(q[b, :, at], k[b, :, at], 1, 1)
             wt = jnp.where(causal, sc, 0.0).astype(BF16)
             w[b, h] = wt
+            qt[b, h] = q[b, :, at].T
             local[b, :, at] = dot(wt, v[b, :, at], 1, 0)
 
     def normalize(s, b):
@@ -230,7 +220,7 @@
             move.start()
         leaving.append(pair)
 
-    pl.semaphore_wait(barrier, 1 + (NX - 1) + (NY - 1) + (NZ - 1))
+    pl.semaphore_wait(barrier, 1 + (plane - 1) + (NZ - 1))
     for move in far_in:
         move.start()
 
@@ -240,31 +230,33 @@
             far_in[i].wait_recv()
 
     ready(0, 1)
-    x_up(0, 0)
+    up(0, 0)
     ready(2, 3)
-    x_up(0, 1)
+    up(0, 1)
     ready(4, 5)
-    middle = (y_up, z_all, y_down, x_down)
+    middle = (z_all, down)
     work = [(s, b) for s in streams for b in range(NC)]
-    local_forward(*work[0])
+    for unit in work[:2]:
+        local_forward(*unit)
     for j, stage in enumerate(middle):
         for s in streams:
             stage(0, s)
-        if j + 1 < len(work):
-            local_forward(*work[j + 1])
+        for unit in work[2:] if j == 0 else ():
+            local_forward(*unit)
     sent = list(pending)
     for s in streams:
         arrive(0, s)
         for b in range(NC):
             normalize(s, b)
-        x_up(1, s)
+        up(1, s)
     leave(6, att, att_out, None)
-    local_backward(*work[0])
+    for unit in work[:2]:
+        local_backward(*unit)
     for j, stage in enumerate(middle):
         for s in streams:
             stage(1, s)
-        if j + 1 < len(work):
-            local_backward(*work[j + 1])
+        for unit in work[2:] if j == 0 else ():
+            local_backward(*unit)
     leave(7, gq, gq_out, None)
     for one in sent:
         one().wait_send()
@@ -307,21 +299,18 @@
     def vm(shape, dtype):
         return pltpu.VMEM(shape, dtype)
 
-    square, strip = per + (NX, DH, DH), per + (NY, chunk, DH)
+    square, strip = per + (NX, DH, DH), per + (NY * NX, chunk, DH)
     scratch = (
         [vm(both, BF16)] * 4
-        + [vm((NC, heads, rows, rows), BF16), vm(both, F32), vm(both, BF16)]
+        + [vm((NC, heads, rows, rows), BF16), vm((NC, heads, DH, rows), BF16), vm(both, F32), vm(both, BF16)]
         + [vm(both, BF16)] * 4
         + [vm(both, F32)] * 2
         + [vm(square, F32), vm(square, BF16)]
-        + [vm(square, BF16)] * 2
-        + [vm(square, F32)]
         + [vm(strip, BF16)] * 2
         + [vm(strip, F32)]
         + [vm(per + (chunk, DH), BF16), vm(per + (NZ, chunk, DH), BF16)]
         + [vm(strip, BF16)] * 2
-        + [vm(square, BF16)] * 2
-        + [pltpu.SemaphoreType.DMA(per + (5,))] * 2
+        + [pltpu.SemaphoreType.DMA(per + (3,))] * 2
         + [pltpu.SemaphoreType.DMA((12,))] * 3
     )
     out = jax.ShapeDtypeStruct((rows, feats), BF16)

time: 68.1 us -> 65.7 us (0.965)
  Pallas kernels: 67.4 us -> 65 us
    pallas_call x1, Pallas kernels: 66 us -> 63.6 us  [body(): pl.pallas_call(kernel, out_shape=(out,) * 4, in_specs=[pl.BlockSpec(memor...]
where the time goes in v4:
time: 65.7 us; the launch traced here: 65.6 us
  Pallas kernels  65 us (99%)
    pallas_call x1, Pallas kernels, body(): pl.pallas_call(kernel, out_shape=(out,) * 4, in_specs=[pl.BlockSpec(memor...  63.6 us
    pallas_call x1, Pallas kernels, body(): pl.pallas_call(hand_over, out_shape=(out,) * 4, in_specs=[pl.BlockSpec(me...  1.35 us

profile of v4, /device:TPU:1, one launch (start us, length us, event | category | flops | bytes accessed | tf_op | source)
XLA Modules:
  0.0 65.6 jit_solution(3043940077860637500)
XLA Ops:
  0.6 63.6 %shard_map.75 = (bf16[128,2048]{1,0:T(8,128)(2,1)S(1)}, bf16[128,2048]{1,0:T(8,128)(2,1)S(1)}, bf16[128,2048]{1,0:T(8,128)(2,1)S(1)}, bf16[128,2048]{1,0:T(8,128)(2,1)S(1)}) custom-call(bf16[128,2048]{1,0:T(8,128)(2,1)} %q_in.1, bf16[128,2048]{1,0:T(8,128)(2,1)} %k_in.1, bf16[128,2048]{1,0:T(8,128)(2,1)} %v_in.1, bf16[128,2048]{1,0:T(8,128)(2,1)} %g_in.1), custom_call_target="tpu_custom_call" | custom-call | flops 805306368 | bytes 4194304 | tf_op jit(solution)/shard_map/pallas_call | solution.py:317
  64.3 1.3 %shard_map.76 = (bf16[128,2048]{1,0:T(8,128)(2,1)}, bf16[128,2048]{1,0:T(8,128)(2,1)}, bf16[128,2048]{1,0:T(8,128)(2,1)}, bf16[128,2048]{1,0:T(8,128)(2,1)}) custom-call(bf16[128,2048]{1,0:T(8,128)(2,1)S(1)} %get-tuple-element.8.a, bf16[128,2048]{1,0:T(8,128)(2,1)S(1)} %get-tuple-element.9.b, bf16[128,2048]{1,0:T(8,128)(2,1)S(1)} %get-tuple-element.10.c, ...), custom_call_target="tpu_custom_call" | custom-call | tf_op jit(solution)/shard_map/pallas_call | solution.py:331

commit v5 on v4

--- a/solution.py
+++ b/solution.py
@@ -8,7 +8,6 @@
 DH = 128
 NZ, NY, NX, NC = 8, 8, 4, 2
 STREAMS = 2
-UNROLL = 1
 EPS = 1e-06
 MESH = pl.DeviceIdType.MESH
 F32 = jnp.float32
@@ -82,6 +81,16 @@
     col_id = lax.broadcasted_iota(jnp.int32, (rows, rows), 1)
     causal = row_id >= col_id
 
+    def hops(step, n):
+        return min(step, n - step)
+
+    steps = [(dy, dx) for dy in range(NY) for dx in range(NX) if (dy, dx) != (0, 0)]
+    steps.sort(key=lambda step: -hops(step[0], NY) - hops(step[1], NX))
+    targets = (
+        [lax.rem(y + dy, NY) * NX + lax.rem(x + dx, NX) for dy, dx in steps],
+        [lax.rem(z + dz, NZ) for dz in sorted(range(1, NZ), key=lambda dz: -hops(dz, NZ))],
+    )
+
     def cols(h):
         return pl.ds(pl.multiple_of(h * DH, DH), DH)
 
@@ -106,13 +115,8 @@
 
     def scatter(src, dst, d, s, r, ring, whole=False):
         place, me, n = rings[ring]
-
-        def send(off, _):
-            to = lax.rem(me + off, n)
+        for to in targets[ring]:
             copy(src if whole else src.at[to], dst.at[me], d, s, r, place(to)).start()
-            return _
-
-        lax.fori_loop(1, n, send, 0, unroll=UNROLL)
         expect(dst, d, s, r, ring)
 
     def order(d, n):

time: 65.7 us -> 60.3 us (0.918)
  Pallas kernels: 65 us -> 59.5 us
    pallas_call x1, Pallas kernels: 63.6 us -> 58.2 us  [body(): pl.pallas_call(kernel, out_shape=(out,) * 4, in_specs=[pl.BlockSpec(memor...]
where the time goes in v5:
time: 60.3 us; the launch traced here: 60.2 us
  Pallas kernels  59.5 us (99%)
  between operations  0.64 us (1%)
    pallas_call x1, Pallas kernels, body(): pl.pallas_call(kernel, out_shape=(out,) * 4, in_specs=[pl.BlockSpec(memor...  58.2 us
    pallas_call x1, Pallas kernels, body(): pl.pallas_call(hand_over, out_shape=(out,) * 4, in_specs=[pl.BlockSpec(me...  1.35 us

profile of v5, /device:TPU:1, one launch (start us, length us, event | category | flops | bytes accessed | tf_op | source)
XLA Modules:
  0.0 60.2 jit_solution(15243191669855245024)
XLA Ops:
  0.6 58.2 %shard_map.75 = (bf16[128,2048]{1,0:T(8,128)(2,1)S(1)}, bf16[128,2048]{1,0:T(8,128)(2,1)S(1)}, bf16[128,2048]{1,0:T(8,128)(2,1)S(1)}, bf16[128,2048]{1,0:T(8,128)(2,1)S(1)}) custom-call(bf16[128,2048]{1,0:T(8,128)(2,1)} %q_in.1, bf16[128,2048]{1,0:T(8,128)(2,1)} %k_in.1, bf16[128,2048]{1,0:T(8,128)(2,1)} %v_in.1, bf16[128,2048]{1,0:T(8,128)(2,1)} %g_in.1), custom_call_target="tpu_custom_call" | custom-call | flops 805306368 | bytes 4194304 | tf_op jit(solution)/shard_map/pallas_call | solution.py:321
  58.8 1.3 %shard_map.76 = (bf16[128,2048]{1,0:T(8,128)(2,1)}, bf16[128,2048]{1,0:T(8,128)(2,1)}, bf16[128,2048]{1,0:T(8,128)(2,1)}, bf16[128,2048]{1,0:T(8,128)(2,1)}) custom-call(bf16[128,2048]{1,0:T(8,128)(2,1)S(1)} %get-tuple-element.8.a, bf16[128,2048]{1,0:T(8,128)(2,1)S(1)} %get-tuple-element.9.b, bf16[128,2048]{1,0:T(8,128)(2,1)S(1)} %get-tuple-element.10.c, ...), custom_call_target="tpu_custom_call" | custom-call | tf_op jit(solution)/shard_map/pallas_call | solution.py:335
